TPU v7x, 32 devices: a whole 2x2x4 slice. The times are simulated.
32 devices in a mesh: grp: 2 (over y), ex: 8 (over z, core), lay: 2 (over x).
Axes of the slice: x: 2, y: 2, z: 4, core: 2. Of those that a mesh axis runs over, the one named last changes fastest.
Arguments:
- train_grads: bfloat16 [2, 8192, 4096], P('lay', ('grp', 'ex')), parts along dimension 1, may hold values from -0.0625 to 0.0625
- query_grads: bfloat16 [2, 512, 4096], P('lay', ('grp', 'ex')), parts along dimension 1, may hold values from -6 to 6
- out_basis: float32 [2, 64, 64], P('lay'), may hold values from -0.75 to 0.75
- in_basis: float32 [2, 64, 64], P('lay'), may hold values from -0.75 to 0.75
- eigenvalues: float32 [2, 64, 64], P('lay'), may hold values from 0.05 to 5
Outputs:
- scores: float32 [8192, 256], P(('grp', 'ex'), 'lay'), parts along dimension 0
There are 2 independent parts, one for each index of `grp`. A program takes and returns all parts, laid end to end along the dimension named above; an argument that names none is the same for every part. Nothing has to cross between parts.
All inputs are finite; a program needn't handle non-finite values.
Results may differ from a plain program's by a relative error of at most 0.0029.
Values may be sent and summed in bfloat16 or wider, within the bound.
A program may use at most 64 MiB of HBM per device.

v0:
```python
import jax
import jax.numpy as jnp
from jax import lax
from jax.sharding import PartitionSpec as P

DAMPING = 0.1


def precondition(queries, out_basis, in_basis, eigenvalues):
    layers, count, width = queries.shape
    outer = out_basis.shape[1]
    grid = queries.astype(jnp.float32).reshape(layers, count, outer, width // outer)
    inner = jnp.einsum("lqac,lcd->lqad", grid, in_basis, precision=lax.Precision.HIGHEST)
    rotated = jnp.einsum("lab,lqad->lqbd", out_basis, inner, precision=lax.Precision.HIGHEST)
    rotated = rotated / (eigenvalues[:, None, :, :] + DAMPING)
    back = jnp.einsum("lqbd,lcd->lqbc", rotated, in_basis, precision=lax.Precision.HIGHEST)
    result = jnp.einsum("lab,lqbc->lqac", out_basis, back, precision=lax.Precision.HIGHEST)
    return result.reshape(layers, count, width).astype(jnp.bfloat16)


def on_device(train_grads, query_grads, out_basis, in_basis, eigenvalues):
    precond = precondition(query_grads, out_basis, in_basis, eigenvalues)
    partial_sums = jnp.einsum(
        "lep,lqp->eq",
        train_grads,
        lax.all_gather(precond, "ex", axis=1, tiled=True),
        preferred_element_type=jnp.float32,
    )
    return lax.psum_scatter(partial_sums, "lay", scatter_dimension=1, tiled=True)


def solution(mesh):
    in_specs = (
        P("lay", ("grp", "ex"), None),
        P("lay", ("grp", "ex"), None),
        P("lay", None, None),
        P("lay", None, None),
        P("lay", None, None),
    )
    out_specs = P(("grp", "ex"), "lay")
    return jax.shard_map(
        on_device, mesh=mesh, in_specs=in_specs, out_specs=out_specs, check_vma=False
    )
```

profile of v0, /device:TPU:0, one launch (start us, length us, event | category | flops | bytes accessed | tf_op | source)
XLA Modules:
  0.0 75.5 jit_solution(892185327320739365)
XLA Ops:
  6.5 0.0 copy-start
  6.5 0.0 copy-start.1
  6.5 0.0 all-gather.2.cloned.1.call-start
  6.5 0.8 %add_bitcast_fusion = f32[64,64]{1,0:T(8,128)S(1)} fusion(f32[1,64,64]{2,1,0:T(8,128)} %param.9), kind=kLoop, calls=%fused_computation.16 | loop fusion | flops 4096 | bytes 32768 | tf_op jit(solution)/shard_map/add | solution.py:15
  7.3 0.1 copy.8
  7.4 1.5 %reshape.56 = bf16[32,64,64]{2,1,0:T(8,128)(2,1)S(1)} reshape(bf16[1,32,4096]{2,1,0:T(8,128)(2,1)} %param.6) | data formatting | bytes 524288 | tf_op jit(solution)/shard_map/reshape
  8.9 0.0 copy-done
  8.9 1.6 %fusion.16 = f32[32,64,64]{1,2,0:T(8,128)S(1)} fusion(bf16[32,64,64]{2,1,0:T(8,128)(2,1)S(1)} %reshape.56, f32[1,64,64]{2,1,0:T(8,128)S(1)} %copy-done), kind=kOutput, calls=%fused_computation.14 | convolution fusion | flops 100663296 | bytes 802816 | tf_op jit(solution)/shard_map/lqac,lcd->lqad/dot_general | solution.py:13
  10.5 1.7 %convolution_bitcast_fusion = f32[1,32,64,64]{2,3,1,0:T(8,128)S(1)} fusion(f32[32,64,64]{1,2,0:T(8,128)S(1)} %fusion.16, f32[1,64,64]{2,1,0:T(8,128)} %param.7), kind=kOutput, calls=%fused_computation.3 | convolution fusion | flops 100663296 | bytes 1064960 | tf_op jit(solution)/shard_map/lab,lqad->lqbd/dot_general | solution.py:14
  12.2 1.1 %fusion.9 = f32[32,64,64]{1,2,0:T(8,128)S(1)} fusion(f32[1,32,64,64]{2,3,1,0:T(8,128)S(1)} %convolution_bitcast_fusion, f32[64,64]{0,1:T(8,128)S(1)} %copy.8, f32[1,64,64]{2,1,0:T(8,128)S(1)} %copy-done), kind=kOutput, calls=%fused_computation.7 | convolution fusion | flops 100794368 | bytes 1081344 | tf_op jit(solution)/shard_map/lqbd,lcd->lqbc/dot_general | solution.py:16
  13.4 0.0 copy-done.1
  13.4 1.0 %fusion.8 = bf16[1,32,64,64]{2,3,1,0:T(8,128)(2,1)S(1)} fusion(f32[32,64,64]{1,2,0:T(8,128)S(1)} %fusion.9, f32[1,64,64]{2,1,0:T(8,128)S(1)} %copy-done.1), kind=kOutput, calls=%fused_computation.6 | convolution fusion | flops 100794368 | bytes 802816 | tf_op jit(solution)/shard_map/lab,lqbc->lqac/dot_general | solution.py:17
  14.3 0.3 copy.9
  14.6 1.2 %convert_element_type.24 = bf16[1,32,4096]{2,1,0:T(8,128)(2,1)} reshape(bf16[1,32,64,64]{3,2,1,0:T(8,128)(2,1)S(1)} %copy.9) | data formatting | bytes 524288 | tf_op jit(solution)/shard_map/convert_element_type | solution.py:18
  15.8 0.0 all-gather.2.cloned.1.call-update
  15.8 0.0 reduce-scatter.2.cloned.1.call-start
  15.9 31.9 %all-gather.2.cloned.1.call-done = bf16[1,256,4096]{2,1,0:T(8,128)(2,1)} async-done(((bf16[1,32,4096]{2,1,0:T(8,128)(2,1)}), bf16[1,256,4096]{2,1,0:T(8,128)(2,1)}) %all-gather.2.cloned.1.call-update) | async-done | bytes 2097168 | tf_op jit(solution)/shard_map/all_gather | solution.py:26
  47.8 4.9 %fusion.3 = f32[512,256]{0,1:T(8,128)} fusion(bf16[1,512,4096]{2,1,0:T(8,128)(2,1)} %param.5, bf16[1,256,4096]{2,1,0:T(8,128)(2,1)} %all-gather.2.cloned.1.call-done), kind=kOutput, calls=%fused_computation.5 | convolution fusion | flops 1073741824 | bytes 6815744 | tf_op jit(solution)/shard_map/lep,lqp->eq/dot_general | solution.py:23
  52.7 0.0 reduce-scatter.2.cloned.1.call-update
  52.7 14.2 %reduce-scatter.2.cloned.1.call-done = f32[512,128]{0,1:T(8,128)} async-done(((f32[512,256]{0,1:T(8,128)}), f32[512,128]{0,1:T(8,128)}) %reduce-scatter.2.cloned.1.call-update) | async-done | bytes 262160 | tf_op jit(solution)/shard_map/reduce_scatter | solution.py:29
  66.9 1.8 %copy.10 = f32[512,128]{1,0:T(8,128)} copy(f32[512,128]{0,1:T(8,128)} %reduce-scatter.2.cloned.1.call-done) | data formatting | bytes 524288 | tf_op jit(solution)/shard_map/reduce_scatter | solution.py:29
Async XLA Ops:
  6.5 2.3 %copy-start = (f32[1,64,64]{2,1,0:T(8,128)S(1)}, f32[1,64,64]{2,1,0:T(8,128)}, u32[]{:S(2)}) copy-start(f32[1,64,64]{2,1,0:T(8,128)} %param.8) | copy-start | bytes 49156
  6.5 6.8 %copy-start.1 = (f32[1,64,64]{2,1,0:T(8,128)S(1)}, f32[1,64,64]{2,1,0:T(8,128)}, u32[]{:S(2)}) copy-start(f32[1,64,64]{2,1,0:T(8,128)} %param.7) | copy-start | bytes 49156
  6.5 41.2 %all-gather.2.cloned.1.call-start = ((), (), s32[]{:S(2)}) async-start(), calls=%async_computation.1 | async-start | bytes 2359296 | tf_op jit(solution)/shard_map/all_gather | solution.py:26
  15.8 51.1 %reduce-scatter.2.cloned.1.call-start = ((), (), s32[]{:S(2)}) async-start(), calls=%async_computation.2 | async-start | bytes 786432 | tf_op jit(solution)/shard_map/reduce_scatter | solution.py:29
Sparse Core Ops, SparseCore 0:
  15.9 31.7 all-gather.1
  52.8 14.0 reduce-scatter.1
where the time goes:
time: 75.8 us; the launch traced here: 75.5 us
  waiting for transfers between devices  46.1 us (61%)
  between operations  13.4 us (18%)
  matrix products  10.3 us (14%)
  local copies, waits for them, and re-layouts  4.8 us (6%)
  other arithmetic  0.77 us (1%)
    all_gather x1, waiting for transfers between devices, on_device(): lax.all_gather(precond, 'ex', axis=1, tiled=True)  31.9 us
    reduce_scatter x1, waiting for transfers between devices, on_device(): lax.psum_scatter(partial_sums, 'lay', scatter_dimension=1, tiled=True)  14.2 us
    dot_general x1, matrix products, on_device(): jnp.einsum('lep,lqp->eq', train_grads, lax.all_gather(precond, 'ex', axis...  4.9 us
    reduce_scatter x1, local copies, waits for them, and re-layouts, on_device(): lax.psum_scatter(partial_sums, 'lay', scatter_dimension=1, tiled=True)  1.78 us
    dot_general x1, matrix products, precondition(): jnp.einsum('lab,lqad->lqbd', out_basis, inner, precision=lax.Precision.HI...  1.72 us
    dot_general x1, matrix products, precondition(): jnp.einsum('lqac,lcd->lqad', grid, in_basis, precision=lax.Precision.HIGH...  1.63 us
  transfers between devices with their start and end apart: 2, of which 2 were waited for; matrix products, arithmetic and copies ran while one was open for 0% of the time, Pallas kernels for 0%

commit v1 on v0

v1 whole, which is shorter than its diff:
```python
import functools

import jax
import jax.numpy as jnp
from jax import lax
from jax.experimental import pallas as pl
from jax.experimental.pallas import tpu as pltpu
from jax.sharding import PartitionSpec as P

DAMPING = 0.1
CORES = 2
CHUNKS = 4
LANES = 128
F32, BF16 = jnp.float32, jnp.bfloat16
NN = (((1,), (0,)), ((), ()))
NT = (((1,), (1,)), ((), ()))


def dot(a, b, dims=NN):
    return lax.dot_general(a, b, dims, preferred_element_type=F32)


def split(x):
    high = x.astype(BF16)
    return high, (x - high.astype(F32)).astype(BF16)


def kernel(z_size, lay_size, train_hbm, query_ref, out_ref, in_ref, eig_ref, score_ref,
           train, held, by_tile, by_query, acc, own, stage, landed,
           train_sem, recv_line, recv_pair, send_line, send_pair, send_lay, recv_lay):
    ex, lay = lax.axis_index("ex"), lax.axis_index("lay")
    z, core = ex // CORES, ex % CORES
    count, width = query_ref.shape[1:]
    side = out_ref.shape[1]
    tiles = width // LANES
    columns = width // CHUNKS
    per_chunk = tiles // CHUNKS
    groups = z_size // lay_size
    has_left, has_right = z > 0, z < z_size - 1

    load = pltpu.make_async_copy(train_hbm.at[0], train, train_sem)
    load.start()

    barrier = pltpu.get_barrier_semaphore()

    def greet(target):
        pl.semaphore_signal(barrier, inc=1, device_id=target, device_id_type=pl.DeviceIdType.MESH)

    pl.when(has_left)(lambda: greet({"ex": ex - CORES}))
    pl.when(has_right)(lambda: greet({"ex": ex + CORES}))
    greet({"ex": z * CORES + 1 - core})
    for step in range(1, lay_size):
        greet({"lay": (lay + step) % lay_size})

    def line_copy(source, chunk, direction):
        block = held.at[source, chunk, pl.ds(pl.multiple_of(core * count, count), count)]
        return pltpu.make_async_remote_copy(
            block, block, send_line.at[source, chunk, (direction + 1) // 2], recv_line.at[source, chunk],
            device_id={"ex": ex + direction * CORES}, device_id_type=pl.DeviceIdType.MESH)

    def pair_copy(source, chunk, who):
        block = held.at[source, chunk, pl.ds(pl.multiple_of(who * count, count), count)]
        return pltpu.make_async_remote_copy(
            block, block, send_pair.at[source, chunk], recv_pair.at[source, chunk],
            device_id={"ex": z * CORES + 1 - core}, device_id_type=pl.DeviceIdType.MESH)

    def lay_copy(source):
        return pltpu.make_async_remote_copy(
            stage.at[source], landed.at[lay, source % groups], send_lay.at[source],
            recv_lay.at[lay, source % groups],
            device_id={"lay": source // groups}, device_id_type=pl.DeviceIdType.MESH)

    half = jnp.concatenate([in_ref[0], in_ref[0]], axis=1)
    low_lane = lax.broadcasted_iota(jnp.int32, half.shape, 1) < side
    zero = jnp.zeros_like(half)
    first, second = jnp.where(low_lane, half, 0.0), jnp.where(low_lane, 0.0, half)
    mix = jnp.concatenate([
        jnp.concatenate([first, zero], axis=1), jnp.concatenate([zero, first], axis=1),
        jnp.concatenate([second, zero], axis=1), jnp.concatenate([zero, second], axis=1)], axis=0)
    mix_high, mix_low = split(mix)
    rows = lax.broadcasted_iota(jnp.int32, (side, side), 0)
    cols = lax.broadcasted_iota(jnp.int32, (side, side), 1)
    order = (cols == 2 * (rows % tiles) + rows // tiles).astype(BF16)
    basis_high, basis_low = split(out_ref[0])
    sorted_high, sorted_low = dot(order, basis_high), dot(order, basis_low)
    to_eigen = jnp.concatenate([sorted_high.T, sorted_high.T, sorted_low.T], axis=1).astype(BF16)
    from_eigen = jnp.concatenate([sorted_high, sorted_high, sorted_low], axis=1).astype(BF16)
    scale = 1.0 / (eig_ref[0] + DAMPING)
    scale = jnp.concatenate([scale] * 4, axis=1)

    for p in range(tiles):
        by_tile[p * count:(p + 1) * count, :] = query_ref[0, :, p * LANES:(p + 1) * LANES].astype(F32)

    def stacked(x):
        high, low = split(x)
        return jnp.concatenate([high, low, high], axis=0)

    for quad in range(count // 4):
        pairs = jnp.concatenate([
            jnp.concatenate([by_tile[pl.ds(4 * quad + 2 * j + i, tiles, stride=count), :] for i in range(2)], axis=1)
            for j in range(2)], axis=0).astype(BF16)
        inner = dot(pairs, mix_high) + dot(pairs, mix_low)
        inner = jnp.concatenate([
            jnp.concatenate([inner[j * tiles:(j + 1) * tiles, s * LANES:(s + 1) * LANES] for j in range(2)], axis=1)
            for s in range(2)], axis=0)
        rotated = dot(to_eigen, stacked(inner)) * scale
        back = dot(from_eigen, stacked(rotated))
        back = jnp.concatenate([
            jnp.concatenate([back[s * tiles:(s + 1) * tiles, j * LANES:(j + 1) * LANES] for s in range(2)], axis=1)
            for j in range(2)], axis=0)
        high, low = split(back)
        result = dot(high, mix_high, NT) + dot(high, mix_low, NT) + dot(low, mix_high, NT)
        for j in range(2):
            for i in range(2):
                at = (4 * quad + 2 * j + i) * tiles
                by_query[at:at + tiles, :] = result[j * tiles:(j + 1) * tiles, i * LANES:(i + 1) * LANES]

    neighbours = has_left.astype(jnp.int32) + has_right.astype(jnp.int32) + lay_size
    pl.semaphore_wait(barrier, neighbours)

    mine = pl.ds(pl.multiple_of(core * count, count), count)
    for chunk in range(CHUNKS):
        for t in range(per_chunk):
            tile = by_query[pl.ds(chunk * per_chunk + t, count, stride=tiles), :]
            held[z, chunk, mine, t * LANES:(t + 1) * LANES] = tile.astype(BF16)
        pl.when(has_left)(lambda: line_copy(z, chunk, -1).start())
        pl.when(has_right)(lambda: line_copy(z, chunk, 1).start())
        pair_copy(z, chunk, core).start()

    def forward(source, chunk, direction, more):
        line_copy(source, chunk, direction).wait_recv()
        pl.when(more)(lambda: line_copy(source, chunk, direction).start())
        pair_copy(source, chunk, core).start()

    def multiply(source, chunk, slot):
        pair_copy(source, chunk, 1 - core).wait_recv()
        part = dot(held[source, chunk], train[:, chunk * columns:(chunk + 1) * columns], NT)
        if chunk > 0:
            part = part + acc[slot]
        if chunk < CHUNKS - 1:
            acc[slot] = part
        else:
            @pl.when(source // groups == lay)
            def _():
                own[source % groups] = part

            @pl.when(source // groups != lay)
            def _():
                stage[source] = part.astype(BF16)
                lay_copy(source).start()

    def multiply_both(distance, chunk):
        pl.when((distance >= 0) & (z + distance < z_size))(lambda: multiply(z + distance, chunk, 0))
        pl.when((distance >= 1) & (z - distance >= 0))(lambda: multiply(z - distance, chunk, 1))

    load.wait()

    def step(distance, carry):
        for chunk in range(CHUNKS):
            @pl.when((distance >= 1) & (z + distance < z_size))
            def _():
                forward(z + distance, chunk, -1, has_left)

            @pl.when((distance >= 1) & (z - distance >= 0))
            def _():
                forward(z - distance, chunk, 1, has_right)

            if chunk == 0:
                multiply_both(distance - 1, CHUNKS - 1)
            else:
                multiply_both(distance, chunk - 1)
        return carry

    lax.fori_loop(0, z_size, step, 0)
    multiply_both(z_size - 1, CHUNKS - 1)

    for peer in range(lay_size):
        @pl.when(peer != lay)
        def _():
            for group in range(groups):
                pltpu.make_async_remote_copy(
                    stage.at[0], landed.at[peer, group], send_lay.at[0], recv_lay.at[peer, group],
                    device_id={"lay": peer}, device_id_type=pl.DeviceIdType.MESH).wait_recv()
                own[group] = own[group] + landed[peer, group].astype(F32)
    total = jnp.concatenate([own[group] for group in range(groups)], axis=0)
    score_ref[...] = total.T

    def drain(source, carry):
        @pl.when(source // groups != lay)
        def _():
            lay_copy(source).wait_send()

        for chunk in range(CHUNKS):
            pair_copy(source, chunk, core).wait_send()
            pl.when(has_left & (source >= z))(lambda: line_copy(source, chunk, -1).wait_send())
            pl.when(has_right & (source <= z))(lambda: line_copy(source, chunk, 1).wait_send())
        return carry

    lax.fori_loop(0, z_size, drain, 0)


def solution(mesh):
    z_size, lay_size = mesh.shape["ex"] // CORES, mesh.shape["lay"]

    def on_device(train_grads, query_grads, out_basis, in_basis, eigenvalues):
        examples, width = train_grads.shape[1:]
        count = query_grads.shape[1]
        both = CORES * count
        groups = z_size // lay_size
        vmem = pl.BlockSpec(memory_space=pltpu.VMEM)
        dma = pltpu.SemaphoreType.DMA
        return pl.pallas_call(
            functools.partial(kernel, z_size, lay_size),
            out_shape=jax.ShapeDtypeStruct((examples, groups * both), F32),
            in_specs=[pl.BlockSpec(memory_space=pl.ANY), vmem, vmem, vmem, vmem],
            out_specs=vmem,
            scratch_shapes=[
                pltpu.VMEM((examples, width), BF16),
                pltpu.VMEM((z_size, CHUNKS, both, width // CHUNKS), BF16),
                pltpu.VMEM((count * width // LANES, LANES), F32),
                pltpu.VMEM((count * width // LANES, LANES), F32),
                pltpu.VMEM((2, both, examples), F32),
                pltpu.VMEM((groups, both, examples), F32),
                pltpu.VMEM((z_size, both, examples), BF16),
                pltpu.VMEM((lay_size, groups, both, examples), BF16),
                dma,
                dma((z_size, CHUNKS)),
                dma((z_size, CHUNKS)),
                dma((z_size, CHUNKS, 2)),
                dma((z_size, CHUNKS)),
                dma((z_size,)),
                dma((lay_size, groups)),
            ],
            compiler_params=pltpu.CompilerParams(
                collective_id=0, has_side_effects=True, vmem_limit_bytes=52 * 1024 * 1024
            ),
        )(train_grads, query_grads, out_basis, in_basis, eigenvalues)

    in_specs = (
        P("lay", ("grp", "ex"), None),
        P("lay", ("grp", "ex"), None),
        P("lay", None, None),
        P("lay", None, None),
        P("lay", None, None),
    )
    out_specs = P(("grp", "ex"), "lay")
    return jax.shard_map(
        on_device, mesh=mesh, in_specs=in_specs, out_specs=out_specs, check_vma=False
    )
```

time: 75.8 us -> 32.1 us (0.42)
  waiting for transfers between devices: 46.1 us -> 0 us
  Pallas kernels: 0 us -> 27.7 us
  between operations: 13.4 us -> 0.01 us
  matrix products: 10.3 us -> 0 us
  local copies, waits for them, and re-layouts: 4.8 us -> 3.93 us
  other arithmetic: 0.77 us -> 0 us
    all_gather x1 -> x0, waiting for transfers between devices: 31.9 us -> none  [on_device(): lax.all_gather(precond, 'ex', axis=1, tiled=True)]
    pallas_call x0 -> x1, Pallas kernels: none -> 27.7 us  [on_device(): pl.pallas_call(functools.partial(kernel, z_size, lay_size), out_shape=jax...]
    reduce_scatter x1 -> x0, waiting for transfers between devices: 14.2 us -> none  [on_device(): lax.psum_scatter(partial_sums, 'lay', scatter_dimension=1, tiled=True)]
    dot_general x5 -> x0, matrix products: 10.3 us -> none  [the longest x1 4.9 us: on_device(): jnp.einsum('lep,lqp->eq', train_grads, lax.all_gather(precond, 'ex', axis...]
    unnamed x4 -> x9, local copies, waits for them, and re-layouts: 0.01 us -> 3.93 us
    reduce_scatter x1 -> x0, local copies, waits for them, and re-layouts: 1.78 us -> none  [on_device(): lax.psum_scatter(partial_sums, 'lay', scatter_dimension=1, tiled=True)]
    reshape x1 -> x0, local copies, waits for them, and re-layouts: 1.48 us -> none
    convert_element_type x2 -> x0, local copies, waits for them, and re-layouts: 1.45 us -> none  [precondition(): return result.reshape(layers, count, width).astype(jnp.bfloat16)]
  transfers between devices with their start and end apart: 2 -> 0, of which waited for: 2 -> 0; matrix products, arithmetic and copies ran while one was open for 0% -> 0% of each run, Pallas kernels for 0% -> 0%
where the time goes in v1:
time: 32.1 us; the launch traced here: 31.7 us
  Pallas kernels  27.7 us (86%)
  local copies, waits for them, and re-layouts  3.93 us (12%)
    pallas_call x1, Pallas kernels, on_device(): pl.pallas_call(functools.partial(kernel, z_size, lay_size), out_shape=jax...  27.7 us
    unnamed x9, local copies, waits for them, and re-layouts  3.93 us

profile of v1, /device:TPU:0, one launch (start us, length us, event | category | flops | bytes accessed | tf_op | source)
XLA Modules:
  0.0 31.7 jit_solution(9157067457955979226)
XLA Ops:
  0.0 0.0 copy-start
  0.0 0.9 %copy-done = bf16[1,32,4096]{2,1,0:T(8,128)(2,1)S(1)} copy-done((bf16[1,32,4096]{2,1,0:T(8,128)(2,1)S(1)}, bf16[1,32,4096]{2,1,0:T(8,128)(2,1)}, u32[]{:S(2)}) %copy-start) | copy-done | bytes 262168
  1.0 0.0 copy-start.1
  1.0 0.8 %copy-done.1 = f32[1,64,64]{2,1,0:T(8,128)S(1)} copy-done((f32[1,64,64]{2,1,0:T(8,128)S(1)}, f32[1,64,64]{2,1,0:T(8,128)}, u32[]{:S(2)}) %copy-start.1) | copy-done | bytes 16408
  1.7 0.0 copy-start.2
  1.7 0.8 %copy-done.2 = f32[1,64,64]{2,1,0:T(8,128)S(1)} copy-done((f32[1,64,64]{2,1,0:T(8,128)S(1)}, f32[1,64,64]{2,1,0:T(8,128)}, u32[]{:S(2)}) %copy-start.2) | copy-done | bytes 16408
  2.5 0.0 copy-start.3
  2.5 0.8 %copy-done.3 = f32[1,64,64]{2,1,0:T(8,128)S(1)} copy-done((f32[1,64,64]{2,1,0:T(8,128)S(1)}, f32[1,64,64]{2,1,0:T(8,128)}, u32[]{:S(2)}) %copy-start.3) | copy-done | bytes 16408
  3.2 27.7 %shard_map.55 = f32[512,128]{1,0:T(8,128)S(1)} custom-call(bf16[1,512,4096]{2,1,0:T(8,128)(2,1)} %train_hbm.1, bf16[1,32,4096]{2,1,0:T(8,128)(2,1)S(1)} %copy-done, f32[1,64,64]{2,1,0:T(8,128)S(1)} %copy-done.1, f32[1,64,64]{2,1,0:T(8,128)S(1)} %copy-done.2, f32[1,64,64]{2,1,0:T(8,128)S(1)} %copy-done.3), custom_call_target="tpu_custom_call" | custom-call | tf_op jit(solution)/shard_map/pallas_call | solution.py:212
  31.0 0.7 %copy.7 = f32[512,128]{1,0:T(8,128)} copy(f32[512,128]{1,0:T(8,128)S(1)} %shard_map.55) | data formatting | bytes 524288
Async XLA Ops:
  0.0 0.9 %copy-start = (bf16[1,32,4096]{2,1,0:T(8,128)(2,1)S(1)}, bf16[1,32,4096]{2,1,0:T(8,128)(2,1)}, u32[]{:S(2)}) copy-start(bf16[1,32,4096]{2,1,0:T(8,128)(2,1)} %query_ref.1) | copy-start | bytes 786436
  1.0 0.8 %copy-start.1 = (f32[1,64,64]{2,1,0:T(8,128)S(1)}, f32[1,64,64]{2,1,0:T(8,128)}, u32[]{:S(2)}) copy-start(f32[1,64,64]{2,1,0:T(8,128)} %out_ref.1) | copy-start | bytes 49156
  1.7 0.8 %copy-start.2 = (f32[1,64,64]{2,1,0:T(8,128)S(1)}, f32[1,64,64]{2,1,0:T(8,128)}, u32[]{:S(2)}) copy-start(f32[1,64,64]{2,1,0:T(8,128)} %in_ref.1) | copy-start | bytes 49156
  2.5 0.8 %copy-start.3 = (f32[1,64,64]{2,1,0:T(8,128)S(1)}, f32[1,64,64]{2,1,0:T(8,128)}, u32[]{:S(2)}) copy-start(f32[1,64,64]{2,1,0:T(8,128)} %eig_ref.1) | copy-start | bytes 49156

commit v2 on v1

--- a/solution.py
+++ b/solution.py
@@ -25,9 +25,9 @@
     return high, (x - high.astype(F32)).astype(BF16)
 
 
-def kernel(z_size, lay_size, train_hbm, query_ref, out_ref, in_ref, eig_ref, score_ref,
-           train, held, by_tile, by_query, acc, own, stage, landed,
-           train_sem, recv_line, recv_pair, send_line, send_pair, send_lay, recv_lay):
+def kernel(z_size, lay_size, train_hbm, query_hbm, out_hbm, in_hbm, eig_hbm, score_ref,
+           train, query_ref, out_ref, in_ref, eig_ref, held, by_tile, by_query, acc, own, stage, landed,
+           load_sem, recv_line, recv_pair, send_line, send_pair, send_lay, recv_lay):
     ex, lay = lax.axis_index("ex"), lax.axis_index("lay")
     z, core = ex // CORES, ex % CORES
     count, width = query_ref.shape[1:]
@@ -38,8 +38,15 @@
     groups = z_size // lay_size
     has_left, has_right = z > 0, z < z_size - 1
 
-    load = pltpu.make_async_copy(train_hbm.at[0], train, train_sem)
-    load.start()
+    late = CHUNKS // 2
+    first_slot, last_slot = lay == 1 // groups, lay == (z_size - 2) // groups
+    send_late_left, send_late_right = (z == 1) & first_slot, (z == z_size - 2) & last_slot
+    get_late_left, get_late_right = (z == z_size - 1) & last_slot, (z == 0) & first_slot
+
+    loads = [pltpu.make_async_copy(*pair, load_sem.at[i]) for i, pair in enumerate((
+        (query_hbm, query_ref), (in_hbm, in_ref), (out_hbm, out_ref), (eig_hbm, eig_ref), (train_hbm.at[0], train)))]
+    for load in loads:
+        load.start()
 
     barrier = pltpu.get_barrier_semaphore()
 
@@ -69,6 +76,9 @@
             stage.at[source], landed.at[lay, source % groups], send_lay.at[source],
             recv_lay.at[lay, source % groups],
             device_id={"lay": source // groups}, device_id_type=pl.DeviceIdType.MESH)
+
+    for load in loads[:-1]:
+        load.wait()
 
     half = jnp.concatenate([in_ref[0], in_ref[0]], axis=1)
     low_lane = lax.broadcasted_iota(jnp.int32, half.shape, 1) < side
@@ -86,7 +96,7 @@
     to_eigen = jnp.concatenate([sorted_high.T, sorted_high.T, sorted_low.T], axis=1).astype(BF16)
     from_eigen = jnp.concatenate([sorted_high, sorted_high, sorted_low], axis=1).astype(BF16)
     scale = 1.0 / (eig_ref[0] + DAMPING)
-    scale = jnp.concatenate([scale] * 4, axis=1)
+    scale = jnp.concatenate([scale] * count, axis=1)
 
     for p in range(tiles):
         by_tile[p * count:(p + 1) * count, :] = query_ref[0, :, p * LANES:(p + 1) * LANES].astype(F32)
@@ -95,25 +105,24 @@
         high, low = split(x)
         return jnp.concatenate([high, low, high], axis=0)
 
-    for quad in range(count // 4):
-        pairs = jnp.concatenate([
-            jnp.concatenate([by_tile[pl.ds(4 * quad + 2 * j + i, tiles, stride=count), :] for i in range(2)], axis=1)
-            for j in range(2)], axis=0).astype(BF16)
-        inner = dot(pairs, mix_high) + dot(pairs, mix_low)
-        inner = jnp.concatenate([
-            jnp.concatenate([inner[j * tiles:(j + 1) * tiles, s * LANES:(s + 1) * LANES] for j in range(2)], axis=1)
-            for s in range(2)], axis=0)
-        rotated = dot(to_eigen, stacked(inner)) * scale
-        back = dot(from_eigen, stacked(rotated))
-        back = jnp.concatenate([
-            jnp.concatenate([back[s * tiles:(s + 1) * tiles, j * LANES:(j + 1) * LANES] for s in range(2)], axis=1)
-            for j in range(2)], axis=0)
-        high, low = split(back)
-        result = dot(high, mix_high, NT) + dot(high, mix_low, NT) + dot(low, mix_high, NT)
-        for j in range(2):
-            for i in range(2):
-                at = (4 * quad + 2 * j + i) * tiles
-                by_query[at:at + tiles, :] = result[j * tiles:(j + 1) * tiles, i * LANES:(i + 1) * LANES]
+    pairs = jnp.concatenate([
+        jnp.concatenate([by_tile[pl.ds(2 * j + i, tiles, stride=count), :] for i in range(2)], axis=1)
+        for j in range(count // 2)], axis=0).astype(BF16)
+    inner = dot(pairs, mix_high) + dot(pairs, mix_low)
+    inner = jnp.concatenate([
+        jnp.concatenate([inner[j * tiles:(j + 1) * tiles, s * LANES:(s + 1) * LANES] for s in range(2)], axis=0)
+        for j in range(count // 2)], axis=1)
+    rotated = dot(to_eigen, stacked(inner)) * scale
+    back = dot(from_eigen, stacked(rotated))
+    back = jnp.concatenate([
+        jnp.concatenate([back[s * tiles:(s + 1) * tiles, j * LANES:(j + 1) * LANES] for s in range(2)], axis=1)
+        for j in range(count // 2)], axis=0)
+    high, low = split(back)
+    result = dot(high, mix_high, NT) + dot(high, mix_low, NT) + dot(low, mix_high, NT)
+    for j in range(count // 2):
+        for i in range(2):
+            at = (2 * j + i) * tiles
+            by_query[at:at + tiles, :] = result[j * tiles:(j + 1) * tiles, i * LANES:(i + 1) * LANES]
 
     neighbours = has_left.astype(jnp.int32) + has_right.astype(jnp.int32) + lay_size
     pl.semaphore_wait(barrier, neighbours)
@@ -123,22 +132,30 @@
         for t in range(per_chunk):
             tile = by_query[pl.ds(chunk * per_chunk + t, count, stride=tiles), :]
             held[z, chunk, mine, t * LANES:(t + 1) * LANES] = tile.astype(BF16)
-        pl.when(has_left)(lambda: line_copy(z, chunk, -1).start())
-        pl.when(has_right)(lambda: line_copy(z, chunk, 1).start())
+        to_left, to_right = has_left, has_right
+        if chunk >= late:
+            to_left, to_right = to_left & jnp.logical_not(send_late_left), to_right & jnp.logical_not(send_late_right)
+        pl.when(to_left)(lambda: line_copy(z, chunk, -1).start())
+        pl.when(to_right)(lambda: line_copy(z, chunk, 1).start())
         pair_copy(z, chunk, core).start()
+
+    def send_late(direction):
+        for chunk in range(late, CHUNKS):
+            line_copy(z, chunk, direction).start()
 
     def forward(source, chunk, direction, more):
         line_copy(source, chunk, direction).wait_recv()
-        pl.when(more)(lambda: line_copy(source, chunk, direction).start())
+        if more is not False:
+            pl.when(more)(lambda: line_copy(source, chunk, direction).start())
         pair_copy(source, chunk, core).start()
 
-    def multiply(source, chunk, slot):
+    def multiply(source, chunk):
         pair_copy(source, chunk, 1 - core).wait_recv()
         part = dot(held[source, chunk], train[:, chunk * columns:(chunk + 1) * columns], NT)
         if chunk > 0:
-            part = part + acc[slot]
+            part = part + acc[source]
         if chunk < CHUNKS - 1:
-            acc[slot] = part
+            acc[source] = part
         else:
             @pl.when(source // groups == lay)
             def _():
@@ -149,22 +166,32 @@
                 stage[source] = part.astype(BF16)
                 lay_copy(source).start()
 
+    def from_right(distance, chunk):
+        there = z + distance < z_size
+        if chunk >= late:
+            there = there & jnp.logical_not(get_late_right & (distance == 1))
+        return there
+
+    def from_left(distance, chunk):
+        there = (distance >= 1) & (z - distance >= 0)
+        if chunk >= late:
+            there = there & jnp.logical_not(get_late_left & (distance == 1))
+        return there
+
     def multiply_both(distance, chunk):
-        pl.when((distance >= 0) & (z + distance < z_size))(lambda: multiply(z + distance, chunk, 0))
-        pl.when((distance >= 1) & (z - distance >= 0))(lambda: multiply(z - distance, chunk, 1))
-
-    load.wait()
+        pl.when((distance >= 0) & from_right(distance, chunk))(lambda: multiply(z + distance, chunk))
+        pl.when(from_left(distance, chunk))(lambda: multiply(z - distance, chunk))
+
+    loads[-1].wait()
 
     def step(distance, carry):
         for chunk in range(CHUNKS):
-            @pl.when((distance >= 1) & (z + distance < z_size))
-            def _():
-                forward(z + distance, chunk, -1, has_left)
-
-            @pl.when((distance >= 1) & (z - distance >= 0))
-            def _():
-                forward(z - distance, chunk, 1, has_right)
-
+            pl.when((distance >= 1) & from_right(distance, chunk))(
+                lambda: forward(z + distance, chunk, -1, has_left))
+            pl.when(from_left(distance, chunk))(lambda: forward(z - distance, chunk, 1, has_right))
+            if chunk == CHUNKS - 1:
+                pl.when(send_late_left & (z + distance == z_size - 1))(lambda: send_late(-1))
+                pl.when(send_late_right & (z - distance == 0))(lambda: send_late(1))
             if chunk == 0:
                 multiply_both(distance - 1, CHUNKS - 1)
             else:
@@ -173,6 +200,15 @@
 
     lax.fori_loop(0, z_size, step, 0)
     multiply_both(z_size - 1, CHUNKS - 1)
+
+    def finish(source, direction):
+        for chunk in range(late, CHUNKS):
+            forward(source, chunk, direction, False)
+        for chunk in range(late, CHUNKS):
+            multiply(source, chunk)
+
+    pl.when(get_late_right)(lambda: finish(z + 1, -1))
+    pl.when(get_late_left)(lambda: finish(z - 1, 1))
 
     for peer in range(lay_size):
         @pl.when(peer != lay)
@@ -207,23 +243,26 @@
         count = query_grads.shape[1]
         both = CORES * count
         groups = z_size // lay_size
-        vmem = pl.BlockSpec(memory_space=pltpu.VMEM)
         dma = pltpu.SemaphoreType.DMA
         return pl.pallas_call(
             functools.partial(kernel, z_size, lay_size),
             out_shape=jax.ShapeDtypeStruct((examples, groups * both), F32),
-            in_specs=[pl.BlockSpec(memory_space=pl.ANY), vmem, vmem, vmem, vmem],
-            out_specs=vmem,
+            in_specs=[pl.BlockSpec(memory_space=pl.ANY)] * 5,
+            out_specs=pl.BlockSpec(memory_space=pltpu.VMEM),
             scratch_shapes=[
                 pltpu.VMEM((examples, width), BF16),
+                pltpu.VMEM(query_grads.shape, BF16),
+                pltpu.VMEM(out_basis.shape, F32),
+                pltpu.VMEM(in_basis.shape, F32),
+                pltpu.VMEM(eigenvalues.shape, F32),
                 pltpu.VMEM((z_size, CHUNKS, both, width // CHUNKS), BF16),
                 pltpu.VMEM((count * width // LANES, LANES), F32),
                 pltpu.VMEM((count * width // LANES, LANES), F32),
-                pltpu.VMEM((2, both, examples), F32),
+                pltpu.VMEM((z_size, both, examples), F32),
                 pltpu.VMEM((groups, both, examples), F32),
                 pltpu.VMEM((z_size, both, examples), BF16),
                 pltpu.VMEM((lay_size, groups, both, examples), BF16),
-                dma,
+                dma((5,)),
                 dma((z_size, CHUNKS)),
                 dma((z_size, CHUNKS)),
                 dma((z_size, CHUNKS, 2)),
@@ -232,7 +271,7 @@
                 dma((lay_size, groups)),
             ],
             compiler_params=pltpu.CompilerParams(
-                collective_id=0, has_side_effects=True, vmem_limit_bytes=52 * 1024 * 1024
+                collective_id=0, has_side_effects=True, vmem_limit_bytes=60 * 1024 * 1024
             ),
         )(train_grads, query_grads, out_basis, in_basis, eigenvalues)
 

time: 32.1 us -> 29.6 us (0.922); the launches traced: 31.7 us -> 29.5 us
  local copies, waits for them, and re-layouts: 3.93 us -> 1.67 us
    unnamed x9 -> x1, local copies, waits for them, and re-layouts: 3.93 us -> 1.67 us
where the time goes in v2:
time: 29.6 us; the launch traced here: 29.5 us
  Pallas kernels  27.8 us (94%)
  local copies, waits for them, and re-layouts  1.67 us (6%)
    pallas_call x1, Pallas kernels, on_device(): pl.pallas_call(functools.partial(kernel, z_size, lay_size), out_shape=jax...  27.8 us
    unnamed x1, local copies, waits for them, and re-layouts  1.67 us

profile of v2, /device:TPU:0, one launch (start us, length us, event | category | flops | bytes accessed | tf_op | source)
XLA Modules:
  0.0 29.5 jit_solution(9776514311591189496)
XLA Ops:
  0.0 27.8 %shard_map.55 = f32[512,128]{1,0:T(8,128)} custom-call(bf16[1,512,4096]{2,1,0:T(8,128)(2,1)} %train_hbm.1, bf16[1,32,4096]{2,1,0:T(8,128)(2,1)} %query_hbm.1, f32[1,64,64]{2,1,0:T(8,128)} %out_hbm.1, f32[1,64,64]{2,1,0:T(8,128)} %in_hbm.1, f32[1,64,64]{2,1,0:T(8,128)} %eig_hbm.1), custom_call_target="tpu_custom_call" | custom-call | tf_op jit(solution)/shard_map/pallas_call | solution.py:247
  27.8 1.7 %copy.7 = f32[512,128]{1,0:T(8,128)} copy(f32[512,128]{1,0:T(8,128)} %shard_map.55) | data formatting | bytes 524288

commit v3 on v2

--- a/solution.py
+++ b/solution.py
@@ -38,7 +38,7 @@
     groups = z_size // lay_size
     has_left, has_right = z > 0, z < z_size - 1
 
-    late = CHUNKS // 2
+    late = CHUNKS - 1
     first_slot, last_slot = lay == 1 // groups, lay == (z_size - 2) // groups
     send_late_left, send_late_right = (z == 1) & first_slot, (z == z_size - 2) & last_slot
     get_late_left, get_late_right = (z == z_size - 1) & last_slot, (z == 0) & first_slot
@@ -246,7 +246,7 @@
         dma = pltpu.SemaphoreType.DMA
         return pl.pallas_call(
             functools.partial(kernel, z_size, lay_size),
-            out_shape=jax.ShapeDtypeStruct((examples, groups * both), F32),
+            out_shape=pltpu.VMEM((examples, groups * both), F32),
             in_specs=[pl.BlockSpec(memory_space=pl.ANY)] * 5,
             out_specs=pl.BlockSpec(memory_space=pltpu.VMEM),
             scratch_shapes=[
@@ -271,7 +271,7 @@
                 dma((lay_size, groups)),
             ],
             compiler_params=pltpu.CompilerParams(
-                collective_id=0, has_side_effects=True, vmem_limit_bytes=60 * 1024 * 1024
+                collective_id=0, has_side_effects=True, vmem_limit_bytes=58 * 1024 * 1024
             ),
         )(train_grads, query_grads, out_basis, in_basis, eigenvalues)
 

time: 29.6 us -> 27.6 us (0.932)
  Pallas kernels: 27.8 us -> 26.7 us
  local copies, waits for them, and re-layouts: 1.67 us -> 0.71 us
    pallas_call x1, Pallas kernels: 27.8 us -> 26.7 us  [on_device(): pl.pallas_call(functools.partial(kernel, z_size, lay_size), out_shape=plt...]
    unnamed x1, local copies, waits for them, and re-layouts: 1.67 us -> 0.71 us
where the time goes in v3:
time: 27.6 us; the launch traced here: 27.4 us
  Pallas kernels  26.7 us (97%)
  local copies, waits for them, and re-layouts  0.71 us (3%)
    pallas_call x1, Pallas kernels, on_device(): pl.pallas_call(functools.partial(kernel, z_size, lay_size), out_shape=plt...  26.7 us
    unnamed x1, local copies, waits for them, and re-layouts  0.71 us

profile of v3, /device:TPU:0, one launch (start us, length us, event | category | flops | bytes accessed | tf_op | source)
XLA Modules:
  0.0 27.4 jit_solution(5579260801196753726)
XLA Ops:
  0.0 26.7 %shard_map.55 = f32[512,128]{1,0:T(8,128)S(1)} custom-call(bf16[1,512,4096]{2,1,0:T(8,128)(2,1)} %train_hbm.1, bf16[1,32,4096]{2,1,0:T(8,128)(2,1)} %query_hbm.1, f32[1,64,64]{2,1,0:T(8,128)} %out_hbm.1, f32[1,64,64]{2,1,0:T(8,128)} %in_hbm.1, f32[1,64,64]{2,1,0:T(8,128)} %eig_hbm.1), custom_call_target="tpu_custom_call" | custom-call | tf_op jit(solution)/shard_map/pallas_call | solution.py:247
  26.7 0.7 %copy.7 = f32[512,128]{1,0:T(8,128)} copy(f32[512,128]{1,0:T(8,128)S(1)} %shard_map.55) | data formatting | bytes 524288

commit v4 on v3

--- a/solution.py
+++ b/solution.py
@@ -26,15 +26,17 @@
 
 
 def kernel(z_size, lay_size, train_hbm, query_hbm, out_hbm, in_hbm, eig_hbm, score_ref,
-           train, query_ref, out_ref, in_ref, eig_ref, held, by_tile, by_query, acc, own, stage, landed,
+           train, query_ref, out_ref, in_ref, eig_ref, raw, held, mix_ref, to_ref, from_ref, scale_ref,
+           by_tile, by_query, acc, own, stage, landed,
            load_sem, recv_line, recv_pair, send_line, send_pair, send_lay, recv_lay):
     ex, lay = lax.axis_index("ex"), lax.axis_index("lay")
     z, core = ex // CORES, ex % CORES
     count, width = query_ref.shape[1:]
     side = out_ref.shape[1]
     tiles = width // LANES
-    columns = width // CHUNKS
-    per_chunk = tiles // CHUNKS
+    part_rows = count // 2
+    columns = width // 2
+    per_chunk = tiles // 2
     groups = z_size // lay_size
     has_left, has_right = z > 0, z < z_size - 1
 
@@ -59,14 +61,17 @@
     for step in range(1, lay_size):
         greet({"lay": (lay + step) % lay_size})
 
-    def line_copy(source, chunk, direction):
-        block = held.at[source, chunk, pl.ds(pl.multiple_of(core * count, count), count)]
+    mine = pl.ds(pl.multiple_of(core * part_rows, part_rows), part_rows)
+
+    def line_copy(source, chunk, direction, own_raw=False):
+        block = raw.at[source, chunk] if chunk < 2 else held.at[source, chunk, mine]
+        start = query_hbm.at[0, pl.ds(0, part_rows), pl.ds(chunk * columns, columns)] if own_raw else block
         return pltpu.make_async_remote_copy(
-            block, block, send_line.at[source, chunk, (direction + 1) // 2], recv_line.at[source, chunk],
+            start, block, send_line.at[source, chunk, (direction + 1) // 2], recv_line.at[source, chunk],
             device_id={"ex": ex + direction * CORES}, device_id_type=pl.DeviceIdType.MESH)
 
     def pair_copy(source, chunk, who):
-        block = held.at[source, chunk, pl.ds(pl.multiple_of(who * count, count), count)]
+        block = held.at[source, chunk, pl.ds(pl.multiple_of(who * part_rows, part_rows), part_rows)]
         return pltpu.make_async_remote_copy(
             block, block, send_pair.at[source, chunk], recv_pair.at[source, chunk],
             device_id={"ex": z * CORES + 1 - core}, device_id_type=pl.DeviceIdType.MESH)
@@ -76,6 +81,12 @@
             stage.at[source], landed.at[lay, source % groups], send_lay.at[source],
             recv_lay.at[lay, source % groups],
             device_id={"lay": source // groups}, device_id_type=pl.DeviceIdType.MESH)
+
+    neighbours = has_left.astype(jnp.int32) + has_right.astype(jnp.int32) + lay_size
+    pl.semaphore_wait(barrier, neighbours)
+    for chunk in range(2):
+        pl.when(has_left)(lambda: line_copy(z, chunk, -1, True).start())
+        pl.when(has_right)(lambda: line_copy(z, chunk, 1, True).start())
 
     for load in loads[:-1]:
         load.wait()
@@ -96,48 +107,51 @@
     to_eigen = jnp.concatenate([sorted_high.T, sorted_high.T, sorted_low.T], axis=1).astype(BF16)
     from_eigen = jnp.concatenate([sorted_high, sorted_high, sorted_low], axis=1).astype(BF16)
     scale = 1.0 / (eig_ref[0] + DAMPING)
-    scale = jnp.concatenate([scale] * count, axis=1)
-
-    for p in range(tiles):
-        by_tile[p * count:(p + 1) * count, :] = query_ref[0, :, p * LANES:(p + 1) * LANES].astype(F32)
+    mix_ref[0], mix_ref[1] = mix_high, mix_low
+    to_ref[...], from_ref[...] = to_eigen, from_eigen
+    scale_ref[...] = jnp.concatenate([scale] * part_rows, axis=1)
 
     def stacked(x):
         high, low = split(x)
         return jnp.concatenate([high, low, high], axis=0)
 
-    pairs = jnp.concatenate([
-        jnp.concatenate([by_tile[pl.ds(2 * j + i, tiles, stride=count), :] for i in range(2)], axis=1)
-        for j in range(count // 2)], axis=0).astype(BF16)
-    inner = dot(pairs, mix_high) + dot(pairs, mix_low)
-    inner = jnp.concatenate([
-        jnp.concatenate([inner[j * tiles:(j + 1) * tiles, s * LANES:(s + 1) * LANES] for s in range(2)], axis=0)
-        for j in range(count // 2)], axis=1)
-    rotated = dot(to_eigen, stacked(inner)) * scale
-    back = dot(from_eigen, stacked(rotated))
-    back = jnp.concatenate([
-        jnp.concatenate([back[s * tiles:(s + 1) * tiles, j * LANES:(j + 1) * LANES] for s in range(2)], axis=1)
-        for j in range(count // 2)], axis=0)
-    high, low = split(back)
-    result = dot(high, mix_high, NT) + dot(high, mix_low, NT) + dot(low, mix_high, NT)
-    for j in range(count // 2):
-        for i in range(2):
-            at = (2 * j + i) * tiles
-            by_query[at:at + tiles, :] = result[j * tiles:(j + 1) * tiles, i * LANES:(i + 1) * LANES]
-
-    neighbours = has_left.astype(jnp.int32) + has_right.astype(jnp.int32) + lay_size
-    pl.semaphore_wait(barrier, neighbours)
-
-    mine = pl.ds(pl.multiple_of(core * count, count), count)
-    for chunk in range(CHUNKS):
-        for t in range(per_chunk):
-            tile = by_query[pl.ds(chunk * per_chunk + t, count, stride=tiles), :]
-            held[z, chunk, mine, t * LANES:(t + 1) * LANES] = tile.astype(BF16)
+    def precondition(source, first_chunk, tile_of):
+        for p in range(tiles):
+            by_tile[p * part_rows:(p + 1) * part_rows, :] = tile_of(p).astype(F32)
+        pairs = jnp.concatenate([
+            jnp.concatenate([by_tile[pl.ds(2 * j + i, tiles, stride=part_rows), :] for i in range(2)], axis=1)
+            for j in range(part_rows // 2)], axis=0).astype(BF16)
+        inner = dot(pairs, mix_ref[0]) + dot(pairs, mix_ref[1])
+        inner = jnp.concatenate([
+            jnp.concatenate([inner[j * tiles:(j + 1) * tiles, s * LANES:(s + 1) * LANES] for s in range(2)], axis=0)
+            for j in range(part_rows // 2)], axis=1)
+        rotated = dot(to_ref[...], stacked(inner)) * scale_ref[...]
+        back = dot(from_ref[...], stacked(rotated))
+        back = jnp.concatenate([
+            jnp.concatenate([back[s * tiles:(s + 1) * tiles, j * LANES:(j + 1) * LANES] for s in range(2)], axis=1)
+            for j in range(part_rows // 2)], axis=0)
+        high, low = split(back)
+        result = dot(high, mix_ref[0], NT) + dot(high, mix_ref[1], NT) + dot(low, mix_ref[0], NT)
+        for j in range(part_rows // 2):
+            for i in range(2):
+                at = (2 * j + i) * tiles
+                by_query[at:at + tiles, :] = result[j * tiles:(j + 1) * tiles, i * LANES:(i + 1) * LANES]
+        for chunk in range(2):
+            for t in range(per_chunk):
+                tile = by_query[pl.ds(chunk * per_chunk + t, part_rows, stride=tiles), :]
+                held[source, first_chunk + chunk, mine, t * LANES:(t + 1) * LANES] = tile.astype(BF16)
+
+    precondition(z, 2, lambda p: query_ref[0, part_rows:, p * LANES:(p + 1) * LANES])
+    for chunk in range(2, CHUNKS):
         to_left, to_right = has_left, has_right
         if chunk >= late:
             to_left, to_right = to_left & jnp.logical_not(send_late_left), to_right & jnp.logical_not(send_late_right)
         pl.when(to_left)(lambda: line_copy(z, chunk, -1).start())
         pl.when(to_right)(lambda: line_copy(z, chunk, 1).start())
         pair_copy(z, chunk, core).start()
+    precondition(z, 0, lambda p: query_ref[0, :part_rows, p * LANES:(p + 1) * LANES])
+    for chunk in range(2):
+        pair_copy(z, chunk, core).start()
 
     def send_late(direction):
         for chunk in range(late, CHUNKS):
@@ -147,24 +161,36 @@
         line_copy(source, chunk, direction).wait_recv()
         if more is not False:
             pl.when(more)(lambda: line_copy(source, chunk, direction).start())
-        pair_copy(source, chunk, core).start()
+        if chunk >= 2:
+            pair_copy(source, chunk, core).start()
+        elif chunk == 1:
+            precondition(source, 0, lambda p: raw[
+                source, p // per_chunk, :, p % per_chunk * LANES:(p % per_chunk + 1) * LANES])
+            for done in range(2):
+                pair_copy(source, done, core).start()
 
     def multiply(source, chunk):
         pair_copy(source, chunk, 1 - core).wait_recv()
-        part = dot(held[source, chunk], train[:, chunk * columns:(chunk + 1) * columns], NT)
-        if chunk > 0:
-            part = part + acc[source]
-        if chunk < CHUNKS - 1:
+        column, half = chunk % 2, chunk // 2
+        part = dot(held[source, chunk], train[:, column * columns:(column + 1) * columns], NT)
+        if column == 0:
             acc[source] = part
         else:
+            part = part + acc[source]
+            pieces = [(slice(who * count + half * part_rows, who * count + (half + 1) * part_rows),
+                       part[who * part_rows:(who + 1) * part_rows]) for who in range(CORES)]
+
             @pl.when(source // groups == lay)
             def _():
-                own[source % groups] = part
+                for at, piece in pieces:
+                    own[source % groups, at] = piece
 
             @pl.when(source // groups != lay)
             def _():
-                stage[source] = part.astype(BF16)
-                lay_copy(source).start()
+                for at, piece in pieces:
+                    stage[source, at] = piece.astype(BF16)
+                if half == 1:
+                    lay_copy(source).start()
 
     def from_right(distance, chunk):
         there = z + distance < z_size
@@ -178,9 +204,9 @@
             there = there & jnp.logical_not(get_late_left & (distance == 1))
         return there
 
-    def multiply_both(distance, chunk):
-        pl.when((distance >= 0) & from_right(distance, chunk))(lambda: multiply(z + distance, chunk))
-        pl.when(from_left(distance, chunk))(lambda: multiply(z - distance, chunk))
+    def multiply_both(distance, chunk, also=True):
+        pl.when(also & (distance >= 0) & from_right(distance, chunk))(lambda: multiply(z + distance, chunk))
+        pl.when(also & from_left(distance, chunk))(lambda: multiply(z - distance, chunk))
 
     loads[-1].wait()
 
@@ -193,9 +219,13 @@
                 pl.when(send_late_left & (z + distance == z_size - 1))(lambda: send_late(-1))
                 pl.when(send_late_right & (z - distance == 0))(lambda: send_late(1))
             if chunk == 0:
-                multiply_both(distance - 1, CHUNKS - 1)
-            else:
-                multiply_both(distance, chunk - 1)
+                multiply_both(distance - 1, 3)
+            elif chunk == 2:
+                multiply_both(distance, 0)
+                multiply_both(distance, 1, distance != 1)
+            elif chunk == 3:
+                multiply_both(distance, 1, distance == 1)
+                multiply_both(distance, 2)
         return carry
 
     lax.fori_loop(0, z_size, step, 0)
@@ -243,6 +273,7 @@
         count = query_grads.shape[1]
         both = CORES * count
         groups = z_size // lay_size
+        side = out_basis.shape[1]
         dma = pltpu.SemaphoreType.DMA
         return pl.pallas_call(
             functools.partial(kernel, z_size, lay_size),
@@ -255,10 +286,15 @@
                 pltpu.VMEM(out_basis.shape, F32),
                 pltpu.VMEM(in_basis.shape, F32),
                 pltpu.VMEM(eigenvalues.shape, F32),
-                pltpu.VMEM((z_size, CHUNKS, both, width // CHUNKS), BF16),
-                pltpu.VMEM((count * width // LANES, LANES), F32),
-                pltpu.VMEM((count * width // LANES, LANES), F32),
-                pltpu.VMEM((z_size, both, examples), F32),
+                pltpu.VMEM((z_size, 2, count // 2, width // 2), BF16),
+                pltpu.VMEM((z_size, CHUNKS, count, width // 2), BF16),
+                pltpu.VMEM((2, 2 * LANES, 2 * LANES), BF16),
+                pltpu.VMEM((side, 3 * side), BF16),
+                pltpu.VMEM((side, 3 * side), BF16),
+                pltpu.VMEM((side, count // 2 * side), F32),
+                pltpu.VMEM((count * width // 2 // LANES, LANES), F32),
+                pltpu.VMEM((count * width // 2 // LANES, LANES), F32),
+                pltpu.VMEM((z_size, count, examples), F32),
                 pltpu.VMEM((groups, both, examples), F32),
                 pltpu.VMEM((z_size, both, examples), BF16),
                 pltpu.VMEM((lay_size, groups, both, examples), BF16),

time: 27.6 us -> 30.6 us (1.11)
  Pallas kernels: 26.7 us -> 29.8 us
    pallas_call x1, Pallas kernels: 26.7 us -> 29.8 us  [on_device(): pl.pallas_call(functools.partial(kernel, z_size, lay_size), out_shape=plt...]
where the time goes in v4:
time: 30.6 us; the launch traced here: 30.5 us
  Pallas kernels  29.8 us (97%)
  local copies, waits for them, and re-layouts  0.71 us (2%)
    pallas_call x1, Pallas kernels, on_device(): pl.pallas_call(functools.partial(kernel, z_size, lay_size), out_shape=plt...  29.8 us
    unnamed x1, local copies, waits for them, and re-layouts  0.71 us

profile of v4, /device:TPU:0, one launch (start us, length us, event | category | flops | bytes accessed | tf_op | source)
XLA Modules:
  0.0 30.5 jit_solution(17632004054949209690)
XLA Ops:
  0.0 29.8 %shard_map.55 = f32[512,128]{1,0:T(8,128)S(1)} custom-call(bf16[1,512,4096]{2,1,0:T(8,128)(2,1)} %train_hbm.1, bf16[1,32,4096]{2,1,0:T(8,128)(2,1)} %query_hbm.1, f32[1,64,64]{2,1,0:T(8,128)} %out_hbm.1, f32[1,64,64]{2,1,0:T(8,128)} %in_hbm.1, f32[1,64,64]{2,1,0:T(8,128)} %eig_hbm.1), custom_call_target="tpu_custom_call" | custom-call | tf_op jit(solution)/shard_map/pallas_call | solution.py:278
  29.8 0.7 %copy.7 = f32[512,128]{1,0:T(8,128)} copy(f32[512,128]{1,0:T(8,128)S(1)} %shard_map.55) | data formatting | bytes 524288

commit v5 on v4

--- a/solution.py
+++ b/solution.py
@@ -170,27 +170,27 @@
                 pair_copy(source, done, core).start()
 
     def multiply(source, chunk):
-        pair_copy(source, chunk, 1 - core).wait_recv()
-        column, half = chunk % 2, chunk // 2
-        part = dot(held[source, chunk], train[:, column * columns:(column + 1) * columns], NT)
+        column = chunk - 2
+        for arrived in (column, chunk):
+            pair_copy(source, arrived, 1 - core).wait_recv()
+        block = jnp.concatenate([held[source, column], held[source, chunk]], axis=0)
+        part = dot(block, train[:, column * columns:(column + 1) * columns], NT)
         if column == 0:
             acc[source] = part
         else:
             part = part + acc[source]
-            pieces = [(slice(who * count + half * part_rows, who * count + (half + 1) * part_rows),
-                       part[who * part_rows:(who + 1) * part_rows]) for who in range(CORES)]
+            part = jnp.concatenate([
+                part[(half * CORES + who) * part_rows:(half * CORES + who + 1) * part_rows]
+                for who in range(CORES) for half in range(2)], axis=0)
 
             @pl.when(source // groups == lay)
             def _():
-                for at, piece in pieces:
-                    own[source % groups, at] = piece
+                own[source % groups] = part
 
             @pl.when(source // groups != lay)
             def _():
-                for at, piece in pieces:
-                    stage[source, at] = piece.astype(BF16)
-                if half == 1:
-                    lay_copy(source).start()
+                stage[source] = part.astype(BF16)
+                lay_copy(source).start()
 
     def from_right(distance, chunk):
         there = z + distance < z_size
@@ -204,9 +204,9 @@
             there = there & jnp.logical_not(get_late_left & (distance == 1))
         return there
 
-    def multiply_both(distance, chunk, also=True):
-        pl.when(also & (distance >= 0) & from_right(distance, chunk))(lambda: multiply(z + distance, chunk))
-        pl.when(also & from_left(distance, chunk))(lambda: multiply(z - distance, chunk))
+    def multiply_both(distance, chunk):
+        pl.when((distance >= 0) & from_right(distance, chunk))(lambda: multiply(z + distance, chunk))
+        pl.when(from_left(distance, chunk))(lambda: multiply(z - distance, chunk))
 
     loads[-1].wait()
 
@@ -220,11 +220,7 @@
                 pl.when(send_late_right & (z - distance == 0))(lambda: send_late(1))
             if chunk == 0:
                 multiply_both(distance - 1, 3)
-            elif chunk == 2:
-                multiply_both(distance, 0)
-                multiply_both(distance, 1, distance != 1)
             elif chunk == 3:
-                multiply_both(distance, 1, distance == 1)
                 multiply_both(distance, 2)
         return carry
 
@@ -294,7 +290,7 @@
                 pltpu.VMEM((side, count // 2 * side), F32),
                 pltpu.VMEM((count * width // 2 // LANES, LANES), F32),
                 pltpu.VMEM((count * width // 2 // LANES, LANES), F32),
-                pltpu.VMEM((z_size, count, examples), F32),
+                pltpu.VMEM((z_size, both, examples), F32),
                 pltpu.VMEM((groups, both, examples), F32),
                 pltpu.VMEM((z_size, both, examples), BF16),
                 pltpu.VMEM((lay_size, groups, both, examples), BF16),

time: 30.6 us -> 27.9 us (0.912)
  Pallas kernels: 29.8 us -> 27.1 us
    pallas_call x1, Pallas kernels: 29.8 us -> 27.1 us  [on_device(): pl.pallas_call(functools.partial(kernel, z_size, lay_size), out_shape=plt...]
where the time goes in v5:
time: 27.9 us; the launch traced here: 27.8 us
  Pallas kernels  27.1 us (97%)
  local copies, waits for them, and re-layouts  0.71 us (3%)
    pallas_call x1, Pallas kernels, on_device(): pl.pallas_call(functools.partial(kernel, z_size, lay_size), out_shape=plt...  27.1 us
    unnamed x1, local copies, waits for them, and re-layouts  0.71 us

profile of v5, /device:TPU:0, one launch (start us, length us, event | category | flops | bytes accessed | tf_op | source)
XLA Modules:
  0.0 27.8 jit_solution(9503666814546369228)
XLA Ops:
  0.0 27.1 %shard_map.55 = f32[512,128]{1,0:T(8,128)S(1)} custom-call(bf16[1,512,4096]{2,1,0:T(8,128)(2,1)} %train_hbm.1, bf16[1,32,4096]{2,1,0:T(8,128)(2,1)} %query_hbm.1, f32[1,64,64]{2,1,0:T(8,128)} %out_hbm.1, f32[1,64,64]{2,1,0:T(8,128)} %in_hbm.1, f32[1,64,64]{2,1,0:T(8,128)} %eig_hbm.1), custom_call_target="tpu_custom_call" | custom-call | tf_op jit(solution)/shard_map/pallas_call | solution.py:274
  27.1 0.7 %copy.7 = f32[512,128]{1,0:T(8,128)} copy(f32[512,128]{1,0:T(8,128)S(1)} %shard_map.55) | data formatting | bytes 524288

commit v6 on v5

--- a/solution.py
+++ b/solution.py
@@ -65,7 +65,7 @@
 
     def line_copy(source, chunk, direction, own_raw=False):
         block = raw.at[source, chunk] if chunk < 2 else held.at[source, chunk, mine]
-        start = query_hbm.at[0, pl.ds(0, part_rows), pl.ds(chunk * columns, columns)] if own_raw else block
+        start = query_ref.at[0, pl.ds(0, part_rows), pl.ds(chunk * columns, columns)] if own_raw else block
         return pltpu.make_async_remote_copy(
             start, block, send_line.at[source, chunk, (direction + 1) // 2], recv_line.at[source, chunk],
             device_id={"ex": ex + direction * CORES}, device_id_type=pl.DeviceIdType.MESH)
@@ -84,11 +84,12 @@
 
     neighbours = has_left.astype(jnp.int32) + has_right.astype(jnp.int32) + lay_size
     pl.semaphore_wait(barrier, neighbours)
+    loads[0].wait()
     for chunk in range(2):
         pl.when(has_left)(lambda: line_copy(z, chunk, -1, True).start())
         pl.when(has_right)(lambda: line_copy(z, chunk, 1, True).start())
 
-    for load in loads[:-1]:
+    for load in loads[1:-1]:
         load.wait()
 
     half = jnp.concatenate([in_ref[0], in_ref[0]], axis=1)

time: 27.9 us -> 27.5 us (0.986)
  Pallas kernels: 27.1 us -> 26.6 us
    pallas_call x1, Pallas kernels: 27.1 us -> 26.6 us  [on_device(): pl.pallas_call(functools.partial(kernel, z_size, lay_size), out_shape=plt...]
where the time goes in v6:
time: 27.5 us; the launch traced here: 27.3 us
  Pallas kernels  26.6 us (97%)
  local copies, waits for them, and re-layouts  0.71 us (3%)
    pallas_call x1, Pallas kernels, on_device(): pl.pallas_call(functools.partial(kernel, z_size, lay_size), out_shape=plt...  26.6 us
    unnamed x1, local copies, waits for them, and re-layouts  0.71 us

profile of v6, /device:TPU:0, one launch (start us, length us, event | category | flops | bytes accessed | tf_op | source)
XLA Modules:
  0.0 27.3 jit_solution(970972402935711757)
XLA Ops:
  0.0 26.6 %shard_map.55 = f32[512,128]{1,0:T(8,128)S(1)} custom-call(bf16[1,512,4096]{2,1,0:T(8,128)(2,1)} %train_hbm.1, bf16[1,32,4096]{2,1,0:T(8,128)(2,1)} %query_hbm.1, f32[1,64,64]{2,1,0:T(8,128)} %out_hbm.1, f32[1,64,64]{2,1,0:T(8,128)} %in_hbm.1, f32[1,64,64]{2,1,0:T(8,128)} %eig_hbm.1), custom_call_target="tpu_custom_call" | custom-call | tf_op jit(solution)/shard_map/pallas_call | solution.py:275
  26.6 0.7 %copy.7 = f32[512,128]{1,0:T(8,128)} copy(f32[512,128]{1,0:T(8,128)S(1)} %shard_map.55) | data formatting | bytes 524288
